TPU v7x, 128 devices: a whole 4x4x4 slice. The times are simulated.
128 devices in a mesh: row: 16 (over x, y_lo, core), col: 8 (over y_hi, z).
Axes of the slice: x: 4, y: 4 (y_hi: 2, y_lo: 2; y = y_hi * 2 + y_lo), z: 4, core: 2. Of those that a mesh axis runs over, the one named last changes fastest.
Arguments:
- a_values: bfloat16 [8192, 8192], P('row', 'col'), may hold values from -0.15625 to 0.15625
- b_values: bfloat16 [8192, 8192], P('row', 'col'), may hold values from -6 to 6
- a_pattern: int32 [64, 64], P('row', 'col'), may hold values from 0 to 1, as said below
- b_pattern: int32 [64, 64], P('row', 'col'), may hold values from 0 to 1, as said below
- c_pattern: int32 [64, 64], P('row', 'col'), may hold values from 0 to 1, as said below
- owner_list: int32 [64], replicated, may hold values from 0 to 63, as said below
Outputs:
- product: bfloat16 [8192, 8192], P('row', 'col')
Inputs may be any that keep to these rules, and one draw needn't show every extreme that they name: a_pattern is 0 or 1 for each block. b_pattern is 0 or 1 for each block. c_pattern is 0 or 1 for each block. owner_list is a permutation of 0 to 63 of the form owner_list[d * 4 + s] = ((d + shift_s) mod 16) * 4 + q_s, with q a permutation of the 4 slots, slots 2p and 2p+1 sharing one shift, the shifts of different pairs distinct and none zero.
All inputs are finite; a program needn't handle non-finite values.
Results may differ from a plain program's by a relative error of at most 0.001.
Values may be sent and summed in bfloat16 or wider, within the bound.
No kernel may reach another device: no remote copies, remote signals or barrier semaphores. Data moves between devices by JAX's collectives and lax.ppermute only.
A program may use at most 128 MiB of HBM per device.

v0:
```python
import jax
import jax.numpy as jnp
from jax import lax
from jax.experimental import pallas as pl
from jax.experimental.pallas import tpu as pltpu
from jax.sharding import Mesh, PartitionSpec as P

SIZES = {"x": 4, "yl": 2, "core": 2, "yh": 2, "z": 4}
ROW = ("x", "yl", "core")
COL = ("yh", "z")
WIDTH = 128
HALVES = 1


def from_ahead(value, axis, by):
    n = SIZES[axis]
    return lax.ppermute(value, axis, [((i + by) % n, i) for i in range(n)])


def shifted(value, axis, count, shift):
    def branch(by):
        perm = [((i + by) % count, i) for i in range(count)]
        return lambda v: lax.ppermute(v, axis, perm)

    return lax.switch(shift - 1, [branch(by) for by in range(1, count)], value)


def mask_kernel(pattern, ref, *outs):
    per = 8 // len(outs)
    for i in range(4):
        for j in range(8):
            block = ref[i * WIDTH : (i + 1) * WIDTH, j * WIDTH : (j + 1) * WIDTH]
            at = j % per
            outs[j // per][i * WIDTH : (i + 1) * WIDTH, at * WIDTH : (at + 1) * WIDTH] = jnp.where(
                pattern[i, j] > 0, block, jnp.zeros_like(block)
            )


def masked(value, pattern, parts):
    out = jax.ShapeDtypeStruct((512, 1024 // parts), jnp.bfloat16)
    vmem = pl.BlockSpec(memory_space=pltpu.VMEM)
    return pl.pallas_call(
        mask_kernel,
        in_specs=[pl.BlockSpec(memory_space=pltpu.SMEM), vmem],
        out_specs=[vmem] * parts,
        out_shape=[out] * parts,
    )(pattern, value)


def local(a, b, a_pattern, b_pattern, c_pattern, owner_list):
    slot_shift = owner_list[:4] // 4 % 16
    slot_source = owner_list[:4] % 4
    yh, z = lax.axis_index("yh").astype(jnp.int32), lax.axis_index("z").astype(jnp.int32)
    own_b = masked(b, b_pattern, HALVES)
    panels = [lax.all_gather(part, ROW, axis=0, tiled=True) for part in own_b]
    (own_a,) = masked(a, a_pattern, 1)

    full = jnp.zeros((512, 8192), jnp.bfloat16)

    def place(full, piece, dy, step, top=0):
        at = ((yh + dy) % 2 * 4 + (z + step) % 4) * 1024
        return lax.dynamic_update_slice(full, piece, (top, at))

    ahead, behind = from_ahead(own_a, "z", 1), from_ahead(own_a, "z", -1)
    side = from_ahead(own_a, "yh", 1)
    side_ahead, side_behind = from_ahead(side, "z", 1), from_ahead(side, "z", -1)
    for dy, value, up, down in ((0, own_a, ahead, behind), (1, side, side_ahead, side_behind)):
        full = place(full, value, dy, 0)
        full = place(full, up, dy, 1)
        full = place(full, down, dy, -1)
        full = place(full, from_ahead(up[:256], "z", 1), dy, 2)
        full = place(full, from_ahead(down[256:], "z", -1), dy, 2, 256)

    out = []
    per = 8 // HALVES
    for h, panel in enumerate(panels):
        part = jnp.dot(full, panel, preferred_element_type=jnp.float32)
        mask = jnp.repeat(jnp.repeat(c_pattern[:, h * per : (h + 1) * per], WIDTH, axis=0), WIDTH, axis=1)
        part = jnp.where(mask > 0, part, jnp.float32(0.0)).astype(jnp.bfloat16)
        moved = []
        for pair in range(2):
            rows = [lax.dynamic_slice_in_dim(part, slot_source[2 * pair + t] * WIDTH, WIDTH, 0) for t in range(2)]
            moved.append(shifted(jnp.concatenate(rows, axis=0), ROW, 16, slot_shift[2 * pair]))
        out.append(jnp.concatenate(moved, axis=0))
    return out[0] if HALVES == 1 else jnp.concatenate(out, axis=1)


def solution(mesh):
    fine = Mesh(mesh.devices.reshape(tuple(SIZES.values())), tuple(SIZES))
    return jax.shard_map(
        local,
        mesh=fine,
        in_specs=(P(ROW, COL),) * 5 + (P(),),
        out_specs=P(ROW, COL),
        check_vma=False,
    )
```

profile of v0, /device:TPU:1, one launch (start us, length us, event | category | flops | bytes accessed | tf_op | source)
XLA Modules:
  0.0 176.9 jit_solution(17479524335994894443)
XLA Ops:
  6.5 2.5 %shard_map.65 = bf16[512,1024]{1,0:T(8,128)(2,1)} custom-call(s32[4,8]{1,0:T(4,128)} %pattern.3, bf16[512,1024]{1,0:T(8,128)(2,1)} %ref.3), custom_call_target="tpu_custom_call" | custom-call | tf_op jit(solution)/shard_map/pallas_call | solution.py:42
  9.1 2.5 %shard_map.64 = bf16[512,1024]{1,0:T(8,128)(2,1)} custom-call(s32[4,8]{1,0:T(4,128)} %pattern.2, bf16[512,1024]{1,0:T(8,128)(2,1)} %ref.2), custom_call_target="tpu_custom_call" | custom-call | tf_op jit(solution)/shard_map/pallas_call | solution.py:42
  11.6 3.7 %collective-permute-start.34 = (bf16[512,1024]{1,0:T(8,128)(2,1)}, bf16[512,1024]{1,0:T(8,128)(2,1)}, u32[]{:S(2)}, u32[]{:S(2)}) collective-permute-start(bf16[512,1024]{1,0:T(8,128)(2,1)} %shard_map.64), channel_id=1, source_target_pairs={{4,0},{0,4},{5,1},{1,5},{6,2},{2,6},{7,3},{3,7},{12,8},{8,12},{13,... | collective-permute-start | bytes 3145736 | tf_op jit(solution)/shard_map/ppermute | solution.py:17
  15.3 3.8 %collective-permute-start.30 = (bf16[512,1024]{1,0:T(8,128)(2,1)}, bf16[512,1024]{1,0:T(8,128)(2,1)}, u32[]{:S(2)}, u32[]{:S(2)}) collective-permute-start(bf16[512,1024]{1,0:T(8,128)(2,1)} %shard_map.64), channel_id=1, source_target_pairs={{1,0},{2,1},{3,2},{0,3},{5,4},{6,5},{7,6},{4,7},{9,8},{10,9},{11,1... | collective-permute-start | bytes 3145736 | tf_op jit(solution)/shard_map/ppermute | solution.py:17
  19.7 33.3 %collective-permute-done.34 = bf16[512,1024]{1,0:T(8,128)(2,1)} collective-permute-done((bf16[512,1024]{1,0:T(8,128)(2,1)}, bf16[512,1024]{1,0:T(8,128)(2,1)}, u32[]{:S(2)}, u32[]{:S(2)}) %collective-permute-start.34) | collective-permute-done | bytes 1048608 | tf_op jit(solution)/shard_map/ppermute | solution.py:17
  53.1 4.6 %collective-permute-start.35 = (bf16[512,1024]{1,0:T(8,128)(2,1)}, bf16[512,1024]{1,0:T(8,128)(2,1)S(1)}, u32[]{:S(2)}, u32[]{:S(2)}) collective-permute-start(bf16[512,1024]{1,0:T(8,128)(2,1)} %collective-permute-done.34), channel_id=1, source_target_pairs={{1,0},{2,1},{3,2},{0,3},{5,4},{6,5},{7,6},{4,7},{9,8},{10,9},{11,1... | collective-permute-start | bytes 3145736 | tf_op jit(solution)/shard_map/ppermute | solution.py:17
  62.4 1.9 %slice.45 = bf16[256,1024]{1,0:T(8,128)(2,1)} slice(bf16[512,1024]{1,0:T(8,128)(2,1)} %collective-permute-done.30), slice={[0:256], [0:1024]} | slice | bytes 1048576 | tf_op jit(solution)/shard_map/slice | solution.py:71
  64.3 2.6 %collective-permute-start.32 = (bf16[256,1024]{1,0:T(8,128)(2,1)}, bf16[256,1024]{1,0:T(8,128)(2,1)}, u32[]{:S(2)}, u32[]{:S(2)}) collective-permute-start(bf16[256,1024]{1,0:T(8,128)(2,1)} %slice.45), channel_id=1, source_target_pairs={{1,0},{2,1},{3,2},{0,3},{5,4},{6,5},{7,6},{4,7},{9,8},{10,9},{11,1... | collective-permute-start | bytes 1572872 | tf_op jit(solution)/shard_map/ppermute | solution.py:17
  68.8 1.1 slice.46
  70.0 4.3 %broadcast_in_dim.15 = bf16[512,8192]{1,0:T(8,128)(2,1)} broadcast(bf16[]{:T(256)} %constant.129.clone.1), dimensions={} | broadcast | bytes 8388610 | tf_op jit(solution)/shard_map/broadcast_in_dim | solution.py:58
  74.3 1.0 constant_dynamic-update-slice_fusion.7
  75.4 2.3 %constant_dynamic-update-slice_fusion.6 = bf16[512,8192]{1,0:T(8,128)(2,1)} fusion(bf16[512,8192]{1,0:T(8,128)(2,1)} %constant_dynamic-update-slice_fusion.7, bf16[512,1024]{1,0:T(8,128)(2,1)} %collective-permute-done.30, s32[]{:T(128)S(6)} %select_n.118), kind=kLoop, calls=%fused_computation.14 | loop fusion | bytes 2097156 | tf_op jit(solution)/shard_map/dynamic_update_slice | solution.py:62
  77.6 2.3 %constant_dynamic-update-slice_fusion.5 = bf16[512,8192]{1,0:T(8,128)(2,1)} fusion(bf16[512,8192]{1,0:T(8,128)(2,1)} %constant_dynamic-update-slice_fusion.6, bf16[512,1024]{1,0:T(8,128)(2,1)} %collective-permute-done.31, s32[]{:T(128)S(6)} %select_n.120), kind=kLoop, calls=%fused_computation.13 | loop fusion | bytes 2097156 | tf_op jit(solution)/shard_map/dynamic_update_slice | solution.py:62
  79.9 7.9 %collective-permute-done.32 = bf16[256,1024]{1,0:T(8,128)(2,1)} collective-permute-done((bf16[256,1024]{1,0:T(8,128)(2,1)}, bf16[256,1024]{1,0:T(8,128)(2,1)}, u32[]{:S(2)}, u32[]{:S(2)}) %collective-permute-start.32) | collective-permute-done | bytes 524320 | tf_op jit(solution)/shard_map/ppermute | solution.py:17
  87.8 2.0 %constant_dynamic-update-slice_fusion.4 = bf16[512,8192]{1,0:T(8,128)(2,1)} fusion(bf16[512,8192]{1,0:T(8,128)(2,1)} %constant_dynamic-update-slice_fusion.5, bf16[256,1024]{1,0:T(8,128)(2,1)} %collective-permute-done.32, s32[]{:T(128)S(6)} %select_n.122), kind=kLoop, calls=%fused_computation.12 | loop fusion | bytes 1048580 | tf_op jit(solution)/shard_map/dynamic_update_slice | solution.py:62
  89.9 3.4 %collective-permute-start.37 = (bf16[256,1024]{1,0:T(8,128)(2,1)S(1)}, bf16[256,1024]{1,0:T(8,128)(2,1)S(1)}, u32[]{:S(2)}, u32[]{:S(2)}) collective-permute-start(bf16[256,1024]{1,0:T(8,128)(2,1)S(1)} %slice.47), channel_id=1, source_target_pairs={{1,0},{2,1},{3,2},{0,3},{5,4},{6,5},{7,6},{4,7},{9,8},{10,9},{11,1... | collective-permute-start | bytes 1572872 | tf_op jit(solution)/shard_map/ppermute | solution.py:17
  93.2 0.9 constant_dynamic-update-slice_fusion.9
  94.2 2.4 %constant_dynamic-update-slice_fusion.3 = bf16[512,8192]{1,0:T(8,128)(2,1)} fusion(bf16[512,8192]{1,0:T(8,128)(2,1)} %constant_dynamic-update-slice_fusion.9, bf16[512,1024]{1,0:T(8,128)(2,1)} %collective-permute-done.34, s32[]{:T(128)S(6)} %select_n.124), kind=kLoop, calls=%fused_computation.11 | loop fusion | bytes 2097156 | tf_op jit(solution)/shard_map/dynamic_update_slice | solution.py:62
  96.6 1.1 constant_dynamic-update-slice_fusion.2
  97.7 1.1 constant_dynamic-update-slice_fusion.1
  98.8 0.8 collective-permute-done.37
  99.7 0.9 constant_dynamic-update-slice_fusion
  100.5 3.3 %collective-permute-done.38 = bf16[256,1024]{1,0:T(8,128)(2,1)S(1)} collective-permute-done((bf16[256,1024]{1,0:T(8,128)(2,1)S(1)}, bf16[256,1024]{1,0:T(8,128)(2,1)S(1)}, u32[]{:S(2)}, u32[]{:S(2)}) %collective-permute-start.38) | collective-permute-done | bytes 524320 | tf_op jit(solution)/shard_map/ppermute | solution.py:17
  103.8 0.9 constant_dynamic-update-slice_fusion.8
  104.7 15.6 %all-gather.2.cloned.1.call-done = bf16[8192,1024]{1,0:T(8,128)(2,1)} async-done(((bf16[512,1024]{1,0:T(8,128)(2,1)}), bf16[8192,1024]{1,0:T(8,128)(2,1)}) %all-gather.2.cloned.1.call-update) | async-done | bytes 16777232 | tf_op jit(solution)/shard_map/all_gather | solution.py:55
  120.3 1.6 broadcast_in_dim.14
  122.0 14.8 %select_convert_fusion = bf16[512,1024]{1,0:T(8,128)(2,1)S(1)} fusion(pred[64,8,8,128]{3,2,1,0:T(8,128)(4,1)S(1)} %bitcast.12, bf16[512,8192]{1,0:T(8,128)(2,1)} %constant_dynamic-update-slice_fusion.8, bf16[8192,1024]{1,0:T(8,128)(2,1)} %all-gather.2.cloned.1.call-done), kind=kOutput, calls=%fused_computation | convolution fusion | flops 8590983168 | bytes 26738688 | tf_op jit(solution)/shard_map/dot_general | solution.py:77
  137.0 16.1 %conditional.2 = (bf16[256,1024]{1,0:T(8,128)(2,1)}) conditional(s32[]{:T(128)} %bitcast, bf16[256,1024]{1,0:T(8,128)(2,1)S(1)} %get-tuple-element.79, bf16[256,1024]{1,0:T(8,128)(2,1)S(1)} %get-tuple-element.79, bf16[256,1024]{1,0:T(8,128)(2,1)S(1)} %get-tuple-element.79, ...), branch_computations={%region_0.1_spmd, %region_1.2_spmd, %region_2.3_spmd, %region_3.4_... | conditional | bytes 2097200 | solution.py:25
  137.1 16.0 %collective-permute-done.8 = bf16[256,1024]{1,0:T(8,128)(2,1)} collective-permute-done((bf16[256,1024]{1,0:T(8,128)(2,1)S(1)}, bf16[256,1024]{1,0:T(8,128)(2,1)}, u32[]{:S(2)}, u32[]{:S(2)}) %collective-permute-start.8) | collective-permute-done | bytes 524320 | tf_op jit(solution)/shard_map/cond/branch_8_fun/ppermute | solution.py:23
  153.1 14.7 %conditional.3 = (bf16[256,1024]{1,0:T(8,128)(2,1)}) conditional(s32[]{:T(128)} %bitcast.4, bf16[256,1024]{1,0:T(8,128)(2,1)S(1)} %get-tuple-element.80, bf16[256,1024]{1,0:T(8,128)(2,1)S(1)} %get-tuple-element.80, bf16[256,1024]{1,0:T(8,128)(2,1)S(1)} %get-tuple-element.80, ...), branch_computations={%region_15.16_spmd, %region_16.17_spmd, %region_17.18_spmd, %regio... | conditional | bytes 2097200 | solution.py:25
  153.1 14.7 %collective-permute-done.24 = bf16[256,1024]{1,0:T(8,128)(2,1)} collective-permute-done((bf16[256,1024]{1,0:T(8,128)(2,1)S(1)}, bf16[256,1024]{1,0:T(8,128)(2,1)}, u32[]{:S(2)}, u32[]{:S(2)}) %collective-permute-start.24) | collective-permute-done | bytes 524320 | tf_op jit(solution)/shard_map/cond/branch_9_fun/ppermute | solution.py:23
  167.8 2.2 %pad_maximum_fusion = bf16[512,1024]{1,0:T(8,128)(2,1)} fusion(bf16[256,1024]{1,0:T(8,128)(2,1)} %get-tuple-element.82, bf16[256,1024]{1,0:T(8,128)(2,1)} %get-tuple-element.81), kind=kLoop, calls=%fused_computation.1 | loop fusion | flops 2097152 | bytes 2097152 | tf_op jit(solution)/shard_map/concatenate | solution.py:84
  (25 shorter events, 3.8 us)
Async XLA Ops:
  6.5 113.8 %all-gather.2.cloned.1.call-start = ((), (), s32[]{:S(2)}) async-start(), calls=%async_computation | async-start | bytes 17825792 | tf_op jit(solution)/shard_map/all_gather | solution.py:55
  11.6 62.8 %copy-start = (bf16[512,1024]{1,0:T(8,128)(2,1)S(1)}, bf16[512,1024]{1,0:T(8,128)(2,1)}, u32[]{:S(2)}) copy-start(bf16[512,1024]{1,0:T(8,128)(2,1)} %shard_map.64) | copy-start | bytes 3145732
  11.6 41.5 %collective-permute-start.34 = (bf16[512,1024]{1,0:T(8,128)(2,1)}, bf16[512,1024]{1,0:T(8,128)(2,1)}, u32[]{:S(2)}, u32[]{:S(2)}) collective-permute-start(bf16[512,1024]{1,0:T(8,128)(2,1)} %shard_map.64), channel_id=1, source_target_pairs={{4,0},{0,4},{5,1},{1,5},{6,2},{2,6},{7,3},{3,7},{12,8},{8,12},{13,... | collective-permute-start | bytes 3145736 | tf_op jit(solution)/shard_map/ppermute | solution.py:17
  15.3 47.1 %collective-permute-start.30 = (bf16[512,1024]{1,0:T(8,128)(2,1)}, bf16[512,1024]{1,0:T(8,128)(2,1)}, u32[]{:S(2)}, u32[]{:S(2)}) collective-permute-start(bf16[512,1024]{1,0:T(8,128)(2,1)} %shard_map.64), channel_id=1, source_target_pairs={{1,0},{2,1},{3,2},{0,3},{5,4},{6,5},{7,6},{4,7},{9,8},{10,9},{11,1... | collective-permute-start | bytes 3145736 | tf_op jit(solution)/shard_map/ppermute | solution.py:17
  19.1 49.8 %collective-permute-start.31 = (bf16[512,1024]{1,0:T(8,128)(2,1)}, bf16[512,1024]{1,0:T(8,128)(2,1)}, u32[]{:S(2)}, u32[]{:S(2)}) collective-permute-start(bf16[512,1024]{1,0:T(8,128)(2,1)} %shard_map.64), channel_id=1, source_target_pairs={{3,0},{0,1},{1,2},{2,3},{7,4},{4,5},{5,6},{6,7},{11,8},{8,9},{9,10... | collective-permute-start | bytes 3145736 | tf_op jit(solution)/shard_map/ppermute | solution.py:17
  53.1 36.8 %collective-permute-start.35 = (bf16[512,1024]{1,0:T(8,128)(2,1)}, bf16[512,1024]{1,0:T(8,128)(2,1)S(1)}, u32[]{:S(2)}, u32[]{:S(2)}) collective-permute-start(bf16[512,1024]{1,0:T(8,128)(2,1)} %collective-permute-done.34), channel_id=1, source_target_pairs={{1,0},{2,1},{3,2},{0,3},{5,4},{6,5},{7,6},{4,7},{9,8},{10,9},{11,1... | collective-permute-start | bytes 3145736 | tf_op jit(solution)/shard_map/ppermute | solution.py:17
  58.4 35.8 %collective-permute-start.36 = (bf16[512,1024]{1,0:T(8,128)(2,1)}, bf16[512,1024]{1,0:T(8,128)(2,1)S(1)}, u32[]{:S(2)}, u32[]{:S(2)}) collective-permute-start(bf16[512,1024]{1,0:T(8,128)(2,1)} %collective-permute-done.34), channel_id=1, source_target_pairs={{3,0},{0,1},{1,2},{2,3},{7,4},{4,5},{5,6},{6,7},{11,8},{8,9},{9,10... | collective-permute-start | bytes 3145736 | tf_op jit(solution)/shard_map/ppermute | solution.py:17
  64.3 23.6 %collective-permute-start.32 = (bf16[256,1024]{1,0:T(8,128)(2,1)}, bf16[256,1024]{1,0:T(8,128)(2,1)}, u32[]{:S(2)}, u32[]{:S(2)}) collective-permute-start(bf16[256,1024]{1,0:T(8,128)(2,1)} %slice.45), channel_id=1, source_target_pairs={{1,0},{2,1},{3,2},{0,3},{5,4},{6,5},{7,6},{4,7},{9,8},{10,9},{11,1... | collective-permute-start | bytes 1572872 | tf_op jit(solution)/shard_map/ppermute | solution.py:17
  69.9 23.3 %collective-permute-start.33 = (bf16[256,1024]{1,0:T(8,128)(2,1)S(1)}, bf16[256,1024]{1,0:T(8,128)(2,1)S(1)}, u32[]{:S(2)}, u32[]{:S(2)}) collective-permute-start(bf16[256,1024]{1,0:T(8,128)(2,1)S(1)} %slice.46), channel_id=1, source_target_pairs={{3,0},{0,1},{1,2},{2,3},{7,4},{4,5},{5,6},{6,7},{11,8},{8,9},{9,10... | collective-permute-start | bytes 1572872 | tf_op jit(solution)/shard_map/ppermute | solution.py:17
  89.9 9.8 %collective-permute-start.37 = (bf16[256,1024]{1,0:T(8,128)(2,1)S(1)}, bf16[256,1024]{1,0:T(8,128)(2,1)S(1)}, u32[]{:S(2)}, u32[]{:S(2)}) collective-permute-start(bf16[256,1024]{1,0:T(8,128)(2,1)S(1)} %slice.47), channel_id=1, source_target_pairs={{1,0},{2,1},{3,2},{0,3},{5,4},{6,5},{7,6},{4,7},{9,8},{10,9},{11,1... | collective-permute-start | bytes 1572872 | tf_op jit(solution)/shard_map/ppermute | solution.py:17
  94.2 9.6 %collective-permute-start.38 = (bf16[256,1024]{1,0:T(8,128)(2,1)S(1)}, bf16[256,1024]{1,0:T(8,128)(2,1)S(1)}, u32[]{:S(2)}, u32[]{:S(2)}) collective-permute-start(bf16[256,1024]{1,0:T(8,128)(2,1)S(1)} %slice.48), channel_id=1, source_target_pairs={{3,0},{0,1},{1,2},{2,3},{7,4},{4,5},{5,6},{6,7},{11,8},{8,9},{9,10... | collective-permute-start | bytes 1572872 | tf_op jit(solution)/shard_map/ppermute | solution.py:17
  137.0 16.1 %collective-permute-start.8 = (bf16[256,1024]{1,0:T(8,128)(2,1)S(1)}, bf16[256,1024]{1,0:T(8,128)(2,1)}, u32[]{:S(2)}, u32[]{:S(2)}) collective-permute-start(bf16[256,1024]{1,0:T(8,128)(2,1)S(1)} %param.8), channel_id=1, source_target_pairs={{72,0},{80,8},{88,16},{96,24},{104,32},{112,40},{120,48},{0,56},{8... | collective-permute-start | bytes 1572872 | tf_op jit(solution)/shard_map/cond/branch_8_fun/ppermute | solution.py:23
  153.1 14.7 %collective-permute-start.24 = (bf16[256,1024]{1,0:T(8,128)(2,1)S(1)}, bf16[256,1024]{1,0:T(8,128)(2,1)}, u32[]{:S(2)}, u32[]{:S(2)}) collective-permute-start(bf16[256,1024]{1,0:T(8,128)(2,1)S(1)} %param.24), channel_id=1, source_target_pairs={{80,0},{88,8},{96,16},{104,24},{112,32},{120,40},{0,48},{8,56},{16... | collective-permute-start | bytes 1572872 | tf_op jit(solution)/shard_map/cond/branch_9_fun/ppermute | solution.py:23
Sparse Core Ops, SparseCore 0:
  9.2 111.0 all-gather.1
where the time goes:
time: 177 us
  waiting for transfers between devices  91.7 us (52%)
  local copies, waits for them, and re-layouts  25.2 us (14%)
  starting transfers between devices  18.4 us (10%)
  between operations  17.4 us (10%)
  matrix products  14.8 us (8%)
  Pallas kernels  5 us (3%)
  other arithmetic  4.33 us (2%)
    ppermute x9, waiting for transfers between devices, from_ahead(): return lax.ppermute(value, axis, [((i + by) % n, i) for i in range(n)])  45.4 us
    ppermute x2, waiting for transfers between devices, branch(): return lambda v: lax.ppermute(v, axis, perm)  30.7 us
    ppermute x9, starting transfers between devices, from_ahead(): return lax.ppermute(value, axis, [((i + by) % n, i) for i in range(n)])  18.4 us
    all_gather x1, waiting for transfers between devices, local(): panels = [lax.all_gather(part, ROW, axis=0, tiled=True) for part in own_b]  15.6 us
    dynamic_update_slice x10, local copies, waits for them, and re-layouts, place(): return lax.dynamic_update_slice(full, piece, (top, at))  14.8 us
    dot_general x1, matrix products, local(): part = jnp.dot(full, panel, preferred_element_type=jnp.float32)  14.8 us
    pallas_call x2, Pallas kernels, masked(): pl.pallas_call(mask_kernel, in_specs=[pl.BlockSpec(memory_space=pltpu.SME...  5 us
    broadcast_in_dim x1, local copies, waits for them, and re-layouts, local(): full = jnp.zeros((512, 8192), jnp.bfloat16)  4.3 us
  transfers between devices with their start and end apart: 12, of which 7 were waited for; matrix products, arithmetic and copies ran while one was open for 14% of the time, Pallas kernels for 1%

commit v1 on v0

v1 whole, which is shorter than its diff:
```python
import jax
import jax.numpy as jnp
from jax import lax
from jax.experimental import pallas as pl
from jax.experimental.pallas import tpu as pltpu
from jax.sharding import Mesh, PartitionSpec as P

SIZES = {"x": 4, "yl": 2, "core": 2, "yh": 2, "z": 4}
ROW = ("x", "yl", "core")
COL = ("yh", "z")
WIDTH = 128
SLICE = 16
CAP = 40
PIECE = 33 * SLICE
PACKED = (CAP + 1) * SLICE
CHUNK = 4
OFFSETS = [(dy, dz) for dy in range(2) for dz in range(4)]


def space(kind):
    return pl.BlockSpec(memory_space=kind)


def from_ahead(value, axis, by):
    n = SIZES[axis]
    return lax.ppermute(value, axis, [((i + by) % n, i) for i in range(n)])


def from_offset(value, offset):
    return lax.ppermute(
        value,
        COL,
        [((y + offset[0]) % 2 * 4 + (z + offset[1]) % 4, y * 4 + z) for y in range(2) for z in range(4)],
    )


def shifted(value, axis, count, shift):
    def branch(by):
        perm = [((i + by) % count, i) for i in range(count)]
        return lambda v: lax.ppermute(v, axis, perm)

    return lax.switch(shift - 1, [branch(by) for by in range(1, count)], value)


def mask_kernel(pattern, ref, out):
    for i in range(4):
        for j in range(8):
            at = (slice(i * WIDTH, (i + 1) * WIDTH), slice(j * WIDTH, (j + 1) * WIDTH))
            block = ref[at]
            out[at] = jnp.where(pattern[i, j] > 0, block, jnp.zeros_like(block))


def masked(value, pattern):
    return pl.pallas_call(
        mask_kernel,
        in_specs=[space(pltpu.SMEM), space(pltpu.VMEM)],
        out_specs=space(pltpu.VMEM),
        out_shape=jax.ShapeDtypeStruct((512, 1024), jnp.bfloat16),
    )(pattern, value)


def flags_as_rows(flags, lane):
    row = jnp.zeros((SLICE, WIDTH), jnp.float32)
    for i in range(4):
        for j in range(8):
            row = jnp.where(lane == i * 8 + j, flags[i, j].astype(jnp.float32), row)
    return row


def cut_kernel(pattern, ref, out):
    lane = lax.broadcasted_iota(jnp.int32, (SLICE, WIDTH), 1)
    row = flags_as_rows(pattern, lane).astype(jnp.bfloat16)
    for m in range(8):
        for i in range(4):
            rows = slice(i * WIDTH + m * SLICE, i * WIDTH + (m + 1) * SLICE)
            for j in range(8):
                at = PIECE * m + (i * 8 + j) * SLICE
                out[at : at + SLICE] = ref[rows, j * WIDTH : (j + 1) * WIDTH]
        out[PIECE * m + 32 * SLICE : PIECE * (m + 1)] = row


def cut(value, pattern):
    return pl.pallas_call(
        cut_kernel,
        in_specs=[space(pltpu.SMEM), space(pltpu.VMEM)],
        out_specs=space(pltpu.VMEM),
        out_shape=jax.ShapeDtypeStruct((8 * PIECE, WIDTH), jnp.bfloat16),
    )(pattern, value)


def pack_a_kernel(slots, c_pattern, pieces, first, second, most, flags_v, flags_s, place_s, sem):
    packed = (first, second)
    for m in range(8):
        row = pieces[PIECE * m + 32 * SLICE : PIECE * (m + 1)].astype(jnp.float32).astype(jnp.int32)
        flags_v[m : m + 1] = row[0:1]
    copy = pltpu.make_async_copy(flags_v, flags_s, sem)
    copy.start()
    copy.wait()
    counts = []
    for pair in range(2):
        count = jnp.int32(0)
        for slot in range(2):
            q = slots[2 * pair + slot]

            def step(k, count, pair=pair, q=q):
                at = q * 8 + k % 8
                here = flags_s[k // 8, at]
                to = jnp.minimum(count, CAP)
                packed[pair][pl.ds(pl.multiple_of(to * SLICE, SLICE), SLICE)] = pieces[
                    pl.ds(pl.multiple_of(k // 8 * PIECE + at * SLICE, SLICE), SLICE)
                ]
                place_s[k // 8, at] = jnp.where(here > 0, to + 1, 0)
                return count + jnp.where(here > 0, 1, 0)

            count = lax.fori_loop(0, 64, step, count, unroll=8)
        counts.append(count)
    copy = pltpu.make_async_copy(place_s, flags_v, sem)
    copy.start()
    copy.wait()
    lane = lax.broadcasted_iota(jnp.int32, (SLICE, WIDTH), 1)
    sub = lax.broadcasted_iota(jnp.int32, (SLICE, WIDTH), 0)
    kept = flags_as_rows(c_pattern, lane)
    place = flags_v[...].astype(jnp.float32)
    place = jnp.where(lane < 32, jnp.concatenate([place, place], axis=0), jnp.float32(0.0))
    header = jnp.where(sub < 8, place, kept).astype(jnp.bfloat16)
    for ref in packed:
        ref[CAP * SLICE : (CAP + 1) * SLICE] = header
    most[...] = jnp.full((8, WIDTH), jnp.maximum(counts[0], counts[1]), jnp.int32)


def pack_a(pieces, slots, c_pattern):
    out = jax.ShapeDtypeStruct((PACKED, WIDTH), jnp.bfloat16)
    return pl.pallas_call(
        pack_a_kernel,
        in_specs=[space(pltpu.SMEM)] * 2 + [space(pltpu.VMEM)],
        out_specs=[space(pltpu.VMEM)] * 3,
        out_shape=[out, out, jax.ShapeDtypeStruct((8, WIDTH), jnp.int32)],
        scratch_shapes=[
            pltpu.VMEM((8, WIDTH), jnp.int32),
            pltpu.SMEM((8, WIDTH), jnp.int32),
            pltpu.SMEM((8, WIDTH), jnp.int32),
            pltpu.SemaphoreType.DMA,
        ],
    )(slots, c_pattern, pieces)


def product_kernel(source, slots, *refs):
    parts, panel, out = refs[:4], refs[4], refs[5]
    header_v, header_s, listed, rhs, lhs, total, sem, b_sem = refs[6:]
    for pair in range(2):
        at = pair * PACKED + CAP * SLICE
        header_v[pair * SLICE : (pair + 1) * SLICE] = parts[0][at : at + SLICE].astype(jnp.float32).astype(jnp.int32)
    copy = pltpu.make_async_copy(header_v, header_s, sem)
    copy.start()
    copy.wait()

    length = jnp.int32(0)
    chunks = []
    for pair in range(2):
        q0, q1 = slots[2 * pair], slots[2 * pair + 1]

        def step(k, length, pair=pair, q0=q0, q1=q1):
            first = header_s[pair * SLICE + k // 8, q0 * 8 + k % 8]
            second = header_s[pair * SLICE + k // 8, q1 * 8 + k % 8]
            listed[0, length] = k
            listed[1, length] = first
            listed[2, length] = second
            return length + jnp.where(first + second > 0, 1, 0)

        length = lax.fori_loop(0, 64, step, length, unroll=8)
        for i in range(CHUNK - 1):
            for n in range(3):
                listed[n, length + i] = 0
        length = (length + CHUNK - 1) // CHUNK * CHUNK
        chunks.append(length // CHUNK)
    total[...] = jnp.zeros_like(total)

    def b_copies(chunk):
        slot = chunk % 2
        return [
            pltpu.make_async_copy(
                panel.at[pl.ds(pl.multiple_of(listed[0, chunk * CHUNK + i] * WIDTH, WIDTH), WIDTH)],
                rhs.at[slot, pl.ds(i * WIDTH, WIDTH)],
                b_sem.at[slot, i],
            )
            for i in range(CHUNK)
        ]

    @pl.when(chunks[1] > 0)
    def _():
        for copy in b_copies(jnp.int32(0)):
            copy.start()

    def multiply(chunk, carry):
        @pl.when(chunk + 1 < chunks[1])
        def _():
            for copy in b_copies(chunk + 1):
                copy.start()

        pair = jnp.where(chunk >= chunks[0], 1, 0)
        for i in range(CHUNK):
            for slot in range(2):
                place = listed[1 + slot, chunk * CHUNK + i]
                at = pair * PACKED + jnp.maximum(place - 1, 0) * SLICE
                for dy in range(2):
                    for step in range(4):
                        value = parts[step][pl.ds(pl.multiple_of(at + dy * 2 * PACKED, SLICE), SLICE)]
                        rows = pl.ds(pl.multiple_of(slot * WIDTH + source[dy * 4 + step] * SLICE, SLICE), SLICE)
                        lhs[rows, i * WIDTH : (i + 1) * WIDTH] = jnp.where(place > 0, value, jnp.zeros_like(value))
        for copy in b_copies(chunk):
            copy.wait()
        for n in range(4):
            cols = slice(n * 256, (n + 1) * 256)
            total[pair, :, cols] += jnp.dot(lhs[...], rhs[chunk % 2, :, cols], preferred_element_type=jnp.float32)
        return carry

    lax.fori_loop(0, chunks[1], multiply, 0)
    for slot in range(4):
        q = slots[slot]
        rows = slice(slot % 2 * WIDTH, (slot % 2 + 1) * WIDTH)
        for j in range(8):
            block = total[slot // 2, rows, j * WIDTH : (j + 1) * WIDTH]
            out[slot * WIDTH : (slot + 1) * WIDTH, j * WIDTH : (j + 1) * WIDTH] = jnp.where(
                header_s[slot // 2 * SLICE + 8, q * 8 + j] > 0, block, jnp.zeros_like(block)
            ).astype(jnp.bfloat16)


def packed_product(parts, panel, source, slots):
    return pl.pallas_call(
        product_kernel,
        in_specs=[space(pltpu.SMEM)] * 2 + [space(pltpu.VMEM)] * 4 + [space(pl.ANY)],
        out_specs=space(pltpu.VMEM),
        out_shape=jax.ShapeDtypeStruct((512, 1024), jnp.bfloat16),
        scratch_shapes=[
            pltpu.VMEM((2 * SLICE, WIDTH), jnp.int32),
            pltpu.SMEM((2 * SLICE, WIDTH), jnp.int32),
            pltpu.SMEM((3, 2 * 64 + 2 * CHUNK), jnp.int32),
            pltpu.VMEM((2, CHUNK * WIDTH, 1024), jnp.bfloat16),
            pltpu.VMEM((2 * WIDTH, CHUNK * WIDTH), jnp.bfloat16),
            pltpu.VMEM((2, 2 * WIDTH, 1024), jnp.float32),
            pltpu.SemaphoreType.DMA,
            pltpu.SemaphoreType.DMA((2, CHUNK)),
        ],
        compiler_params=pltpu.CompilerParams(vmem_limit_bytes=24 * 2**20),
    )(source, slots, *parts, panel)


def dense_product(a, a_pattern, c_pattern, panel, slots, slot_shift, source):
    value = masked(a, a_pattern)
    moved, kept = [], []
    for pair in range(2):
        rows = [lax.dynamic_slice_in_dim(value, slots[2 * pair + t] * WIDTH, WIDTH, 0) for t in range(2)]
        flags = [lax.dynamic_slice_in_dim(c_pattern, slots[2 * pair + t], 1, 0) for t in range(2)]
        moved.append(shifted(jnp.concatenate(rows, axis=0), ROW, 16, slot_shift[2 * pair]))
        kept.append(shifted(jnp.concatenate(flags, axis=0), ROW, 16, slot_shift[2 * pair]))
    value = jnp.concatenate(moved, axis=0)
    full = jnp.zeros((512, 8192), jnp.bfloat16)
    for t, offset in enumerate(OFFSETS):
        piece = from_offset(value, offset) if t else value
        full = lax.dynamic_update_slice(full, piece, (0, source[t] * 1024))
    product = jnp.dot(full, panel, preferred_element_type=jnp.float32)
    mask = jnp.repeat(jnp.repeat(jnp.concatenate(kept, axis=0), WIDTH, axis=0), WIDTH, axis=1)
    return jnp.where(mask > 0, product, jnp.float32(0.0)).astype(jnp.bfloat16)


def local(a, b, a_pattern, b_pattern, c_pattern, owner_list):
    slot_shift = owner_list[:4] // 4 % 16
    slots = owner_list[:4] % 4
    yh, z = lax.axis_index("yh").astype(jnp.int32), lax.axis_index("z").astype(jnp.int32)
    ahead = jnp.stack([(yh + dy) % 2 * 4 + (z + dz) % 4 for dy, dz in OFFSETS])
    own_b = masked(b, b_pattern)
    panel = lax.all_gather(own_b, ROW, axis=0, tiled=True)
    a, _ = lax.optimization_barrier((a, own_b))

    pieces = lax.all_to_all(cut(a, a_pattern), COL, 0, 0, tiled=True)
    first, second, most = pack_a(pieces, slots, c_pattern)
    for axis, by in (("x", 2), ("x", 1), ("yl", 1), ("core", 1)):
        most = jnp.maximum(most, from_ahead(most, axis, by))
    first = shifted(first, ROW, 16, slot_shift[0])
    second = shifted(second, ROW, 16, slot_shift[2])
    own = jnp.concatenate([first, second], axis=0)
    both = jnp.concatenate([own, from_ahead(own, "yh", 1)], axis=0)
    parts = [both] + [from_ahead(both, "z", step) for step in (1, 2, 3)]
    return lax.cond(
        most[0, 0] > CAP,
        lambda: dense_product(a, a_pattern, c_pattern, panel, slots, slot_shift, ahead),
        lambda: packed_product(parts, panel, ahead, slots),
    )


def solution(mesh):
    fine = Mesh(mesh.devices.reshape(tuple(SIZES.values())), tuple(SIZES))
    return jax.shard_map(
        local,
        mesh=fine,
        in_specs=(P(ROW, COL),) * 5 + (P(),),
        out_specs=P(ROW, COL),
        check_vma=False,
    )
```

time: 177 us -> 151 us (0.85)
  local copies, waits for them, and re-layouts: 25.2 us -> 3.24 us
  Pallas kernels: 5 us -> 24.5 us
  matrix products: 14.8 us -> 0 us
  waiting for transfers between devices: 91.7 us -> 86.1 us
  between operations: 17.4 us -> 15.3 us
    all_to_all x0 -> x1, waiting for transfers between devices: none -> 22.5 us  [local(): pieces = lax.all_to_all(cut(a, a_pattern), COL, 0, 0, tiled=True)]
    pallas_call x2 -> x4, Pallas kernels: 5 us -> 24.5 us  [the longest x1 12.8 us: packed_product(): pl.pallas_call(product_kernel, in_specs=[space(pltpu.SMEM)] * 2 + [space(...]
    dynamic_update_slice x10 -> x0, local copies, waits for them, and re-layouts: 14.8 us -> none  [place(): return lax.dynamic_update_slice(full, piece, (top, at))]
    dot_general x1 -> x0, matrix products: 14.8 us -> none  [local(): part = jnp.dot(full, panel, preferred_element_type=jnp.float32)]
    ppermute x9 -> x8, waiting for transfers between devices: 45.4 us -> 32 us  [from_ahead(): return lax.ppermute(value, axis, [((i + by) % n, i) for i in range(n)])]
    all_to_all x0 -> x1, starting transfers between devices: none -> 8.49 us  [local(): pieces = lax.all_to_all(cut(a, a_pattern), COL, 0, 0, tiled=True)]
    ppermute x9 -> x8, starting transfers between devices: 18.4 us -> 10.1 us  [from_ahead(): return lax.ppermute(value, axis, [((i + by) % n, i) for i in range(n)])]
    ppermute x2, waiting for transfers between devices: 30.7 us -> 22.9 us  [branch(): return lambda v: lax.ppermute(v, axis, perm)]
  transfers between devices with their start and end apart: 12 -> 12, of which waited for: 7 -> 11; matrix products, arithmetic and copies ran while one was open for 14% -> 3% of each run, Pallas kernels for 1% -> 6%
where the time goes in v1:
time: 151 us
  waiting for transfers between devices  86.1 us (57%)
  Pallas kernels  24.5 us (16%)
  starting transfers between devices  18.7 us (12%)
  between operations  15.3 us (10%)
  other arithmetic  3.43 us (2%)
  local copies, waits for them, and re-layouts  3.24 us (2%)
    ppermute x8, waiting for transfers between devices, from_ahead(): return lax.ppermute(value, axis, [((i + by) % n, i) for i in range(n)])  32 us
    ppermute x2, waiting for transfers between devices, branch(): return lambda v: lax.ppermute(v, axis, perm)  22.9 us
    all_to_all x1, waiting for transfers between devices, local(): pieces = lax.all_to_all(cut(a, a_pattern), COL, 0, 0, tiled=True)  22.5 us
    pallas_call x1, Pallas kernels, packed_product(): pl.pallas_call(product_kernel, in_specs=[space(pltpu.SMEM)] * 2 + [space(...  12.8 us
    ppermute x8, starting transfers between devices, from_ahead(): return lax.ppermute(value, axis, [((i + by) % n, i) for i in range(n)])  10.1 us
    all_gather x1, waiting for transfers between devices, local(): panel = lax.all_gather(own_b, ROW, axis=0, tiled=True)  8.61 us
    all_to_all x1, starting transfers between devices, local(): pieces = lax.all_to_all(cut(a, a_pattern), COL, 0, 0, tiled=True)  8.49 us
    pallas_call x1, Pallas kernels, pack_a(): pl.pallas_call(pack_a_kernel, in_specs=[space(pltpu.SMEM)] * 2 + [space(p...  6.7 us
  transfers between devices with their start and end apart: 12, of which 11 were waited for; matrix products, arithmetic and copies ran while one was open for 3% of the time, Pallas kernels for 6%

profile of v1, /device:TPU:1, one launch (start us, length us, event | category | flops | bytes accessed | tf_op | source)
XLA Modules:
  0.0 151.5 jit_solution(18312139113444264025)
XLA Ops:
  6.5 2.6 %shard_map.66 = bf16[512,1024]{1,0:T(8,128)(2,1)} custom-call(s32[4,8]{1,0:T(4,128)} %pattern.2, bf16[512,1024]{1,0:T(8,128)(2,1)} %ref.1), custom_call_target="tpu_custom_call" | custom-call | tf_op jit(solution)/shard_map/pallas_call | solution.py:54
  9.2 2.4 %shard_map.67 = bf16[4224,128]{1,0:T(8,128)(2,1)} custom-call(s32[4,8]{1,0:T(4,128)} %pattern.3, bf16[512,1024]{1,0:T(8,128)(2,1)} %ref.2), custom_call_target="tpu_custom_call" | custom-call | tf_op jit(solution)/shard_map/pallas_call | solution.py:83
  11.6 8.5 %all-to-all-start = ((bf16[8,528,128]{2,1,0:T(8,128)(2,1)}), bf16[8,528,128]{2,1,0:T(8,128)(2,1)S(1)}, u32[]{:S(2)}, u32[]{:S(2)}) async-start(bf16[8,528,128]{2,1,0:T(8,128)(2,1)} %bitcast.25), calls=%async_computation | async-start | bytes 2162688 | tf_op jit(solution)/shard_map/all_to_all | solution.py:275
  20.1 0.7 and_select_fusion
  20.7 0.6 fusion.3
  22.5 22.5 %all-to-all-done = bf16[8,528,128]{2,1,0:T(8,128)(2,1)S(1)} async-done(((bf16[8,528,128]{2,1,0:T(8,128)(2,1)}), bf16[8,528,128]{2,1,0:T(8,128)(2,1)S(1)}, u32[]{:S(2)}, u32[]{:S(2)}) %all-to-all-start) | async-done | bytes 1081376 | tf_op jit(solution)/shard_map/all_to_all | solution.py:275
  45.0 1.0 copy-done
  46.0 6.7 %shard_map.68 = (bf16[656,128]{1,0:T(8,128)(2,1)S(1)}, bf16[656,128]{1,0:T(8,128)(2,1)S(1)}, s32[8,128]{1,0:T(8,128)}) custom-call(s32[4]{0:T(128)S(1)} %and_select_fusion.2.slots, s32[4,8]{1,0:T(4,128)} %c_pattern.1, bf16[4224,128]{1,0:T(8,128)(2,1)} %bitcast.26), custom_call_target="tpu_custom_call" | custom-call | tf_op jit(solution)/shard_map/pallas_call | solution.py:133
  52.7 10.7 %conditional.7 = (bf16[656,128]{1,0:T(8,128)(2,1)}) conditional(s32[]{:T(128)} %bitcast.18, bf16[656,128]{1,0:T(8,128)(2,1)S(1)} %get-tuple-element.263, bf16[656,128]{1,0:T(8,128)(2,1)S(1)} %get-tuple-element.263, bf16[656,128]{1,0:T(8,128)(2,1)S(1)} %get-tuple-element.263, ...), branch_computations={%region_0.1_spmd, %region_1.2_spmd, %region_2.3_spmd, %region_3.4_... | conditional | bytes 671792 | solution.py:42
  52.8 10.6 %collective-permute-done.12 = bf16[656,128]{1,0:T(8,128)(2,1)} collective-permute-done((bf16[656,128]{1,0:T(8,128)(2,1)S(1)}, bf16[656,128]{1,0:T(8,128)(2,1)}, u32[]{:S(2)}, u32[]{:S(2)}) %collective-permute-start.12) | collective-permute-done | bytes 167968 | tf_op jit(solution)/shard_map/cond/branch_12_fun/ppermute | solution.py:40
  63.4 12.3 %conditional.8 = (bf16[656,128]{1,0:T(8,128)(2,1)}) conditional(s32[]{:T(128)} %bitcast.19, bf16[656,128]{1,0:T(8,128)(2,1)S(1)} %get-tuple-element.264, bf16[656,128]{1,0:T(8,128)(2,1)S(1)} %get-tuple-element.264, bf16[656,128]{1,0:T(8,128)(2,1)S(1)} %get-tuple-element.264, ...), branch_computations={%region_15.16_spmd, %region_16.17_spmd, %region_17.18_spmd, %regio... | conditional | bytes 671792 | solution.py:42
  63.4 12.3 %collective-permute-done.23 = bf16[656,128]{1,0:T(8,128)(2,1)} collective-permute-done((bf16[656,128]{1,0:T(8,128)(2,1)S(1)}, bf16[656,128]{1,0:T(8,128)(2,1)}, u32[]{:S(2)}, u32[]{:S(2)}) %collective-permute-start.23) | collective-permute-done | bytes 167968 | tf_op jit(solution)/shard_map/cond/branch_8_fun/ppermute | solution.py:40
  75.8 1.0 pad_maximum_fusion.4
  76.9 17.6 %collective-permute-done.101 = bf16[1312,128]{1,0:T(8,128)(2,1)S(1)} collective-permute-done((bf16[1312,128]{1,0:T(8,128)(2,1)S(1)}, bf16[1312,128]{1,0:T(8,128)(2,1)S(1)}, u32[]{:S(2)}, u32[]{:S(2)}) %collective-permute-start.101) | collective-permute-done | bytes 335904 | tf_op jit(solution)/shard_map/ppermute | solution.py:26
  94.5 1.0 pad_maximum_fusion.3
  95.5 2.3 %collective-permute-start.102 = (bf16[2624,128]{1,0:T(8,128)(2,1)S(1)}, bf16[2624,128]{1,0:T(8,128)(2,1)S(1)}, u32[]{:S(2)}, u32[]{:S(2)}) collective-permute-start(bf16[2624,128]{1,0:T(8,128)(2,1)S(1)} %pad_maximum_fusion.3), channel_id=1, source_target_pairs={{1,0},{2,1},{3,2},{0,3},{5,4},{6,5},{7,6},{4,7},{9,8},{10,9},{11,1... | collective-permute-start | bytes 2015240 | tf_op jit(solution)/shard_map/ppermute | solution.py:26
  97.8 0.6 collective-permute-start.103
  98.5 0.6 collective-permute-start.104
  99.0 4.5 %collective-permute-done.97 = s32[8,128]{1,0:T(8,128)S(1)} collective-permute-done((s32[8,128]{1,0:T(8,128)}, s32[8,128]{1,0:T(8,128)S(1)}, u32[]{:S(2)}, u32[]{:S(2)}) %collective-permute-start.97) | collective-permute-done | bytes 4128 | tf_op jit(solution)/shard_map/ppermute | solution.py:26
  103.5 0.7 max.12
  104.2 2.2 %collective-permute-start.98 = (s32[8,128]{1,0:T(8,128)S(1)}, s32[8,128]{1,0:T(8,128)S(1)}, u32[]{:S(2)}, u32[]{:S(2)}) collective-permute-start(s32[8,128]{1,0:T(8,128)S(1)} %max.12), channel_id=1, source_target_pairs={{32,0},{64,32},{96,64},{0,96},{33,1},{65,33},{97,65},{1,97},{34,2}... | collective-permute-start | bytes 12296 | tf_op jit(solution)/shard_map/ppermute | solution.py:26
  106.4 0.8 collective-permute-done.98
  107.2 2.9 %collective-permute-done.99 = s32[8,128]{1,0:T(8,128)S(1)} collective-permute-done((s32[8,128]{1,0:T(8,128)S(1)}, s32[8,128]{1,0:T(8,128)S(1)}, u32[]{:S(2)}, u32[]{:S(2)}) %collective-permute-start.99) | collective-permute-done | bytes 4128 | tf_op jit(solution)/shard_map/ppermute | solution.py:26
  110.1 4.3 %collective-permute-start.100 = (s32[8,128]{1,0:T(8,128)S(1)}, s32[8,128]{1,0:T(8,128)S(1)}, u32[]{:S(2)}, u32[]{:S(2)}) collective-permute-start(s32[8,128]{1,0:T(8,128)S(1)} %max.14), channel_id=1, source_target_pairs={{8,0},{0,8},{9,1},{1,9},{10,2},{2,10},{11,3},{3,11},{12,4},{4,12},... | collective-permute-start | bytes 12296 | tf_op jit(solution)/shard_map/ppermute | solution.py:26
  114.4 0.7 collective-permute-done.100
  115.2 0.6 slice.38
  116.5 8.6 %all-gather.2.cloned.1.call-done = bf16[8192,1024]{1,0:T(8,128)(2,1)} async-done(((bf16[512,1024]{1,0:T(8,128)(2,1)}), bf16[8192,1024]{1,0:T(8,128)(2,1)}) %all-gather.2.cloned.1.call-update) | async-done | bytes 16777232 | tf_op jit(solution)/shard_map/all_gather | solution.py:272
  125.1 1.5 collective-permute-done.102
  126.5 4.1 %collective-permute-done.104 = bf16[2624,128]{1,0:T(8,128)(2,1)} collective-permute-done((bf16[2624,128]{1,0:T(8,128)(2,1)S(1)}, bf16[2624,128]{1,0:T(8,128)(2,1)}, u32[]{:S(2)}, u32[]{:S(2)}) %collective-permute-start.104) | collective-permute-done | bytes 671776 | tf_op jit(solution)/shard_map/ppermute | solution.py:26
  130.6 13.0 %conditional.9 = (bf16[512,1024]{1,0:T(8,128)(2,1)S(1)}) conditional(s32[]{:T(128)} %bitcast.9, (s32[8]{0:T(128)S(1)}, s32[4]{0:T(128)S(1)}, bf16[2624,128]{1,0:T(8,128)(2,1)S(1)}, bf16[2624,128]{1,0:T(8,128)(2,1)S(1)}, bf16[2624,128]{1,0:T(8,128)(2,1)S(1)}, /*index=5*/bf16[2624,128]{1,0:T(8,128)(2,1)}, bf16[8192,1024]{1,0:T(8,128)(2,1)}) %tuple.283, ...), branch_computations={%region_30.31_spmd, %region_31.92_spmd} | conditional | flops 8595177472 | bytes 91236840 | solution.py:284
  130.6 12.8 %branch_0_fun.1 = bf16[512,1024]{1,0:T(8,128)(2,1)S(1)} custom-call(s32[8]{0:T(128)S(1)} %get-tuple-element.236.source, s32[4]{0:T(128)S(1)} %get-tuple-element.237.slots, bf16[2624,128]{1,0:T(8,128)(2,1)S(1)} %get-tuple-element.238.refs_0_, bf16[2624,128]{1,0:T(8,128)(2,1)S(1)} %get-tuple-element.239.refs_1_, ...), custom_call_target="tpu_custom_call" | custom-call | tf_op jit(solution)/shard_map/cond/branch_0_fun/pallas_call | solution.py:229
  143.7 1.0 copy-done.2
  (21 shorter events, 0.3 us)
Async XLA Ops:
  6.5 124.1 %copy-start.1 = (bf16[512,1024]{1,0:T(8,128)(2,1)S(1)}, bf16[512,1024]{1,0:T(8,128)(2,1)}, u32[]{:S(2)}) copy-start(bf16[512,1024]{1,0:T(8,128)(2,1)} %ref.2) | copy-start | bytes 3145732
  6.5 124.1 %copy-start.3 = (s32[4,8]{1,0:T(4,128)S(1)}, s32[4,8]{1,0:T(4,128)}, u32[]{:S(2)}) copy-start(s32[4,8]{1,0:T(4,128)} %pattern.3) | copy-start | bytes 388
  6.5 124.1 %copy-start.4 = (s32[4,8]{1,0:T(4,128)S(1)}, s32[4,8]{1,0:T(4,128)}, u32[]{:S(2)}) copy-start(s32[4,8]{1,0:T(4,128)} %c_pattern.1) | copy-start | bytes 388
  6.5 118.5 %all-gather.2.cloned.1.call-start = ((), (), s32[]{:S(2)}) async-start(), calls=%async_computation.1 | async-start | bytes 17825792 | tf_op jit(solution)/shard_map/all_gather | solution.py:272
  11.6 33.4 %all-to-all-start = ((bf16[8,528,128]{2,1,0:T(8,128)(2,1)}), bf16[8,528,128]{2,1,0:T(8,128)(2,1)S(1)}, u32[]{:S(2)}, u32[]{:S(2)}) async-start(bf16[8,528,128]{2,1,0:T(8,128)(2,1)} %bitcast.25), calls=%async_computation | async-start | bytes 2162688 | tf_op jit(solution)/shard_map/all_to_all | solution.py:275
  45.0 1.0 copy-start
  52.7 10.7 %collective-permute-start.12 = (bf16[656,128]{1,0:T(8,128)(2,1)S(1)}, bf16[656,128]{1,0:T(8,128)(2,1)}, u32[]{:S(2)}, u32[]{:S(2)}) collective-permute-start(bf16[656,128]{1,0:T(8,128)(2,1)S(1)} %param.12), channel_id=1, source_target_pairs={{104,0},{112,8},{120,16},{0,24},{8,32},{16,40},{24,48},{32,56},{40... | collective-permute-start | bytes 503816 | tf_op jit(solution)/shard_map/cond/branch_12_fun/ppermute | solution.py:40
  63.4 12.3 %collective-permute-start.23 = (bf16[656,128]{1,0:T(8,128)(2,1)S(1)}, bf16[656,128]{1,0:T(8,128)(2,1)}, u32[]{:S(2)}, u32[]{:S(2)}) collective-permute-start(bf16[656,128]{1,0:T(8,128)(2,1)S(1)} %param.23), channel_id=1, source_target_pairs={{72,0},{80,8},{88,16},{96,24},{104,32},{112,40},{120,48},{0,56},{8... | collective-permute-start | bytes 503816 | tf_op jit(solution)/shard_map/cond/branch_8_fun/ppermute | solution.py:40
  76.8 17.7 %collective-permute-start.101 = (bf16[1312,128]{1,0:T(8,128)(2,1)S(1)}, bf16[1312,128]{1,0:T(8,128)(2,1)S(1)}, u32[]{:S(2)}, u32[]{:S(2)}) collective-permute-start(bf16[1312,128]{1,0:T(8,128)(2,1)S(1)} %pad_maximum_fusion.4), channel_id=1, source_target_pairs={{4,0},{0,4},{5,1},{1,5},{6,2},{2,6},{7,3},{3,7},{12,8},{8,12},{13,... | collective-permute-start | bytes 1007624 | tf_op jit(solution)/shard_map/ppermute | solution.py:26
  95.5 31.0 %collective-permute-start.102 = (bf16[2624,128]{1,0:T(8,128)(2,1)S(1)}, bf16[2624,128]{1,0:T(8,128)(2,1)S(1)}, u32[]{:S(2)}, u32[]{:S(2)}) collective-permute-start(bf16[2624,128]{1,0:T(8,128)(2,1)S(1)} %pad_maximum_fusion.3), channel_id=1, source_target_pairs={{1,0},{2,1},{3,2},{0,3},{5,4},{6,5},{7,6},{4,7},{9,8},{10,9},{11,1... | collective-permute-start | bytes 2015240 | tf_op jit(solution)/shard_map/ppermute | solution.py:26
  97.8 28.7 %collective-permute-start.103 = (bf16[2624,128]{1,0:T(8,128)(2,1)S(1)}, bf16[2624,128]{1,0:T(8,128)(2,1)S(1)}, u32[]{:S(2)}, u32[]{:S(2)}) collective-permute-start(bf16[2624,128]{1,0:T(8,128)(2,1)S(1)} %pad_maximum_fusion.3), channel_id=1, source_target_pairs={{2,0},{3,1},{0,2},{1,3},{6,4},{7,5},{4,6},{5,7},{10,8},{11,9},{8,1... | collective-permute-start | bytes 2015240 | tf_op jit(solution)/shard_map/ppermute | solution.py:26
  98.5 32.1 %collective-permute-start.104 = (bf16[2624,128]{1,0:T(8,128)(2,1)S(1)}, bf16[2624,128]{1,0:T(8,128)(2,1)}, u32[]{:S(2)}, u32[]{:S(2)}) collective-permute-start(bf16[2624,128]{1,0:T(8,128)(2,1)S(1)} %pad_maximum_fusion.3), channel_id=1, source_target_pairs={{3,0},{0,1},{1,2},{2,3},{7,4},{4,5},{5,6},{6,7},{11,8},{8,9},{9,10... | collective-permute-start | bytes 2015240 | tf_op jit(solution)/shard_map/ppermute | solution.py:26
  99.0 4.5 %collective-permute-start.97 = (s32[8,128]{1,0:T(8,128)}, s32[8,128]{1,0:T(8,128)S(1)}, u32[]{:S(2)}, u32[]{:S(2)}) collective-permute-start(s32[8,128]{1,0:T(8,128)} %get-tuple-element.262), channel_id=1, source_target_pairs={{64,0},{96,32},{0,64},{32,96},{65,1},{97,33},{1,65},{33,97},{66,2}... | collective-permute-start | bytes 12296 | tf_op jit(solution)/shard_map/ppermute | solution.py:26
  104.2 3.0 %collective-permute-start.98 = (s32[8,128]{1,0:T(8,128)S(1)}, s32[8,128]{1,0:T(8,128)S(1)}, u32[]{:S(2)}, u32[]{:S(2)}) collective-permute-start(s32[8,128]{1,0:T(8,128)S(1)} %max.12), channel_id=1, source_target_pairs={{32,0},{64,32},{96,64},{0,96},{33,1},{65,33},{97,65},{1,97},{34,2}... | collective-permute-start | bytes 12296 | tf_op jit(solution)/shard_map/ppermute | solution.py:26
  107.2 2.9 %collective-permute-start.99 = (s32[8,128]{1,0:T(8,128)S(1)}, s32[8,128]{1,0:T(8,128)S(1)}, u32[]{:S(2)}, u32[]{:S(2)}) collective-permute-start(s32[8,128]{1,0:T(8,128)S(1)} %max.13), channel_id=1, source_target_pairs={{16,0},{0,16},{17,1},{1,17},{18,2},{2,18},{19,3},{3,19},{20,4},{4,... | collective-permute-start | bytes 12296 | tf_op jit(solution)/shard_map/ppermute | solution.py:26
  110.1 5.1 %collective-permute-start.100 = (s32[8,128]{1,0:T(8,128)S(1)}, s32[8,128]{1,0:T(8,128)S(1)}, u32[]{:S(2)}, u32[]{:S(2)}) collective-permute-start(s32[8,128]{1,0:T(8,128)S(1)} %max.14), channel_id=1, source_target_pairs={{8,0},{0,8},{9,1},{1,9},{10,2},{2,10},{11,3},{3,11},{12,4},{4,12},... | collective-permute-start | bytes 12296 | tf_op jit(solution)/shard_map/ppermute | solution.py:26
  143.7 1.0 copy-start.2
Sparse Core Ops, SparseCore 0:
  9.3 115.7 all-gather.1
